TPU v7x, 256 devices: a whole 4x4x8 slice. The times are simulated.
256 devices in a mesh: elem: 16 (over x_hi, y, core), freq: 16 (over x_lo, z).
Axes of the slice: x: 4 (x_hi: 2, x_lo: 2; x = x_hi * 2 + x_lo), y: 4, z: 8, core: 2. Of those that a mesh axis runs over, the one named last changes fastest.
Arguments:
- stress_modes: bfloat16 [3, 3000, 65536], P(None, None, ('elem', 'freq')), may hold values from -0.109375 to 0.109375
- node_shapes: float32 [4096, 3000], P(('elem', 'freq')), may hold values from -6 to 6
- wheel_nodes: int32 [4], replicated, may hold values from 0 to 4095
- mode_freq: float32 [3000], replicated, may hold values from 0.02 to 1.2
- mode_damping: float32 [3000], replicated, may hold values from 0.01 to 0.08
- freq_bins: int32 [384], P('freq'), may hold values from 1 to 4096
- delay_phase: int32 [4, 384], P(None, 'freq'), may hold values from 0 to 63
- road_psd: float32 [2, 384], P(None, 'freq'), may hold values from 0.05 to 1
- elem_block: int32 [65536], P(('elem', 'freq')), may hold values from 0 to 63
- block_scale: float32 [64], replicated, may hold values from 0.5 to 2
Outputs:
- spectra: bfloat16 [384, 9, 65536], P('freq', None, 'elem')
- moments: float32 [4, 65536], P(None, ('elem', 'freq'))
All inputs are finite; a program needn't handle non-finite values.
Results may differ from a plain program's by a relative error of at most 0.0051.
Values may be sent and summed in bfloat16 or wider, within the bound.
A program may use at most 64 MiB of HBM per device.

v0:
```python
import math

import jax
import jax.numpy as jnp
from jax import lax
from jax.sharding import PartitionSpec as P

NBINS = 4096
PHASES = 64


def excitation(freq_bins, delay_phase, road_psd):
    line_ratio = freq_bins.astype(jnp.float32) / NBINS
    amplitude = jnp.repeat(jnp.sqrt(road_psd), 2, axis=0)
    angles = 2.0 * math.pi / PHASES * delay_phase.astype(jnp.float32)
    return jnp.concatenate(
        [line_ratio[None, :], amplitude * jnp.cos(angles), amplitude * jnp.sin(angles)], axis=0
    )


def responses(factors, wheel_rows, mode_freq, mode_damping):
    line_ratio = factors[0][:, None]
    natural = mode_freq[None, :]
    detune = natural * natural - line_ratio * line_ratio
    damped = 2.0 * mode_damping[None, :] * natural * line_ratio
    magnitude = detune * detune + damped * damped
    gain_real = natural * natural * detune / magnitude
    gain_imag = -natural * natural * damped / magnitude
    columns = []
    for which_track in range(2):
        front_wheel = 2 * which_track
        rear_wheel = 2 * which_track + 1
        drive_real = (
            factors[1 + front_wheel][:, None] * wheel_rows[front_wheel][None, :]
            + factors[1 + rear_wheel][:, None] * wheel_rows[rear_wheel][None, :]
        )
        drive_imag = -(
            factors[5 + front_wheel][:, None] * wheel_rows[front_wheel][None, :]
            + factors[5 + rear_wheel][:, None] * wheel_rows[rear_wheel][None, :]
        )
        columns.append(gain_real * drive_real - gain_imag * drive_imag)
        columns.append(gain_real * drive_imag + gain_imag * drive_real)
    return jnp.stack(columns, axis=1).astype(jnp.bfloat16)


def stress_scaling(elem_block, block_scale):
    matches = elem_block[None, :] == jnp.arange(block_scale.shape[0], dtype=jnp.int32)[:, None]
    return jnp.sum(jnp.where(matches, block_scale[:, None], 0.0), axis=0)


def spectra_of(stress):
    real_part = stress[:, 0::2]
    imag_part = stress[:, 1::2]

    def cross_real(first_comp, second_comp):
        return jnp.sum(
            real_part[:, :, first_comp] * real_part[:, :, second_comp]
            + imag_part[:, :, first_comp] * imag_part[:, :, second_comp],
            axis=1,
        )

    def cross_imag(first_comp, second_comp):
        return jnp.sum(
            imag_part[:, :, first_comp] * real_part[:, :, second_comp]
            - real_part[:, :, first_comp] * imag_part[:, :, second_comp],
            axis=1,
        )

    return jnp.stack(
        [
            cross_real(0, 0),
            cross_real(1, 1),
            cross_real(2, 2),
            cross_real(0, 1),
            cross_real(0, 2),
            cross_real(1, 2),
            cross_imag(0, 1),
            cross_imag(0, 2),
            cross_imag(1, 2),
        ],
        axis=1,
    )


def local(
    stress_modes,
    node_shapes,
    wheel_nodes,
    mode_freq,
    mode_damping,
    freq_bins,
    delay_phase,
    road_psd,
    elem_block,
    block_scale,
):
    rows_here = node_shapes.shape[0]
    first_row = lax.axis_index(("elem", "freq")) * rows_here
    local_rows = wheel_nodes - first_row
    inside = (local_rows >= 0) & (local_rows < rows_here)
    picked = jnp.take(node_shapes, jnp.clip(local_rows, 0, rows_here - 1), axis=0)
    picked = jnp.where(inside[:, None], picked, 0.0)
    wheel_rows = lax.psum(picked, ("elem", "freq"))
    own_factors = excitation(freq_bins, delay_phase, road_psd)
    factors = lax.all_gather(own_factors, "freq", axis=1, tiled=True)
    scaling = stress_scaling(elem_block, block_scale)
    modal = responses(factors, wheel_rows, mode_freq, mode_damping)
    stress = jnp.einsum("fkm,cme->fkce", modal, stress_modes, preferred_element_type=jnp.float32)
    stress = stress * scaling
    normal_x = stress[:, :, 0]
    normal_y = stress[:, :, 1]
    shear = stress[:, :, 2]
    equivalent = jnp.sum(
        normal_x * normal_x + normal_y * normal_y - normal_x * normal_y + 3.0 * shear * shear,
        axis=1,
    )
    line_ratio = factors[0]
    listed = [
        jnp.sum((line_ratio**exponent)[:, None] * equivalent, axis=0) / line_ratio.shape[0]
        for exponent in (0, 1, 2, 4)
    ]
    moments = jnp.stack(listed, axis=0)
    moved = lax.all_to_all(stress, "freq", split_axis=0, concat_axis=3, tiled=True)
    spectra = spectra_of(moved).astype(jnp.bfloat16)
    return (spectra, moments)


def solution(mesh):
    placed = (
        P(None, None, ("elem", "freq")),
        P(("elem", "freq"), None),
        P(),
        P(),
        P(),
        P("freq"),
        P(None, "freq"),
        P(None, "freq"),
        P(("elem", "freq")),
        P(),
    )
    return jax.shard_map(
        local,
        mesh=mesh,
        in_specs=placed,
        out_specs=(P("freq", None, "elem"), P(None, ("elem", "freq"))),
        check_vma=False,
    )
```

profile of v0, /device:TPU:1, one launch (start us, length us, event | category | flops | bytes accessed | tf_op | source)
XLA Modules:
  0.0 259.6 jit_solution(2581913661013369197)
XLA Ops:
  0.6 0.0 copy-start
  0.7 0.7 multiply_bitcast_fusion
  1.3 0.7 sqrt.3
  2.0 0.7 compare_and_fusion
  2.7 0.0 copy-done
  2.7 0.6 gather_fusion
  3.3 0.1 select_select_fusion
  3.4 81.6 %psum.7 = f32[4,3000]{1,0:T(4,128)S(1)} all-reduce(f32[4,3000]{1,0:T(4,128)S(1)} %select_select_fusion), channel_id=1, replica_groups=mesh['elem'=16,'freq'=16] {'elem','freq'}, use_global_device_ids=true, to_apply=%region_0.1 | all-reduce | flops 12000 | bytes 96000 | tf_op jit(solution)/shard_map/psum | solution.py:103
  85.0 0.7 cosine_multiply_fusion
  85.8 24.0 %all-gather = f32[16,24,9]{1,2,0:T(8,128)S(1)} all-gather(f32[1,24,9]{1,2,0:T(8,128)S(1)} %maximum_bitcast_fusion.4), channel_id=1, replica_groups=mesh['elem'=16,'freq'=16] {'freq'}, dimensions={0}, use_global_device_ids=true | all-gather | bytes 14688 | tf_op jit(solution)/shard_map/all_gather | solution.py:105
  109.8 0.1 reshape.1504
  109.9 0.1 slice_reduce_fusion.7
  109.9 0.0 slice-start
  109.9 0.9 select_reduce_fusion
  110.9 1.0 negate_multiply_fusion
  111.8 0.0 slice-start.1
  111.8 7.1 %subtract_convert_fusion.1 = (bf16[384,1,3000]{0,2,1:T(8,128)(2,1)S(1)}, bf16[384,1,3000]{0,2,1:T(8,128)(2,1)S(1)}, bf16[384,1,3000]{0,2,1:T(8,128)(2,1)S(1)}, bf16[384,1,3000]{0,2,1:T(8,128)(2,1)S(1)}) fusion(f32[384]{0:T(512)S(1)} %get-tuple-element.21, f32[384]{0:T(512)S(1)} %get-tuple-element.22, f32[3000]{0:T(1024)S(1)} %bitcast.75, ...), kind=kLoop, calls=%fused_computation.23 | loop fusion | flops 44928000 | bytes 9315360 | tf_op jit(solution)/shard_map/convert.18
  119.0 0.0 slice-done
  119.0 0.0 slice-done.1
  119.0 8.7 %fusion.11 = f32[384,4,3,256]{3,0,2,1:T(8,128)S(1)} fusion(bf16[3,3000,256]{2,1,0:T(8,128)(2,1)S(1)} %bitcast.82, bf16[384,1,3000]{0,2,1:T(8,128)(2,1)S(1)} %get-tuple-element.41, bf16[384,1,3000]{0,2,1:T(8,128)(2,1)S(1)} %get-tuple-element.42, bf16[384,1,3000]{0,2,1:T(8,128)(2,1)S(1)} %get-tuple-element.34, ...), kind=kOutput, calls=%fused_computation.26 | convolution fusion | flops 7115931648 | bytes 18543616 | tf_op jit(solution)/shard_map/fkm,cme->fkce/dot_general | solution.py:108
  127.8 0.0 copy-start.1
  127.8 2.2 copy-done.1
  130.0 5.2 %copy.29 = f32[384,4,3,256]{3,1,2,0:T(4,128)} copy(f32[384,4,3,256]{3,0,2,1:T(8,128)S(1)} %fusion.11) | data formatting | bytes 9437184 | tf_op jit(solution)/shard_map/mul | solution.py:109
  135.2 4.8 %all-to-all-start = ((f32[384,4,3,256]{3,1,2,0:T(4,128)}), f32[384,4,3,256]{3,1,2,0:T(4,128)}, u32[]{:S(2)}, u32[]{:S(2)}) async-start(f32[384,4,3,256]{3,1,2,0:T(4,128)} %copy.29), calls=%async_computation | async-start | bytes 9437184 | tf_op jit(solution)/shard_map/all_to_all | solution.py:123
  140.0 2.9 %fusion.16 = (f32[256]{0:T(256)S(1)}, f32[384,256]{1,0:T(8,128)S(1)}) fusion(f32[384,4,3,256]{3,0,2,1:T(8,128)} %copy-done.1), kind=kLoop, calls=%fused_computation.83 | loop fusion | flops 3833600 | bytes 5112832 | tf_op jit(solution)/shard_map/reduce_sum | solution.py:119
  142.9 0.2 multiply_reduce_fusion.2
  143.2 0.6 pad_maximum_fusion
  143.8 97.3 %all-to-all-done = f32[384,4,3,256]{3,1,2,0:T(4,128)} async-done(((f32[384,4,3,256]{3,1,2,0:T(4,128)}), f32[384,4,3,256]{3,1,2,0:T(4,128)}, u32[]{:S(2)}, u32[]{:S(2)}) %all-to-all-start) | async-done | bytes 4718624 | tf_op jit(solution)/shard_map/all_to_all | solution.py:123
  241.0 7.2 %copy.37 = f32[16,24,4,3,256]{4,0,1,3,2:T(8,128)} copy(f32[16,24,4,3,256]{4,2,3,1,0:T(4,128)} %bitcast.12) | data formatting | bytes 9437184 | tf_op jit(solution)/shard_map/all_to_all | solution.py:123
  248.3 6.0 %all_to_all.16 = f32[24,4,3,4096]{3,0,2,1:T(8,128)} reshape(f32[24,4,3,16,256]{4,3,0,2,1:T(8,128)} %bitcast.70) | data formatting | bytes 9437184 | tf_op jit(solution)/shard_map/all_to_all | solution.py:123
  254.3 2.9 %fusion.17 = (f32[24,2,3,4096]{3,0,2,1:T(8,128)S(1)}, f32[24,2,3,4096]{3,0,2,1:T(8,128)S(1)}) fusion(f32[24,4,3,4096]{3,0,2,1:T(8,128)} %all_to_all.16), kind=kLoop, calls=%fused_computation.84 | loop fusion | bytes 9437184 | tf_op jit(solution)/shard_map/slice | solution.py:52
  257.1 1.0 subtract_reduce_fusion
  258.4 0.0 copy-start.2
  258.4 1.2 copy-done.2
  (19 shorter events, 0.2 us)
Async XLA Ops:
  0.6 2.1 copy-start
  109.9 9.1 %slice-start = ((s8[4608000]{0:T(1024)(128)(4,1)}), s8[4194304]{0:T(1024)(128)(4,1)S(1)}, s32[]{:S(2)}) async-start(s8[4608000]{0:T(1024)(128)(4,1)} %bitcast.81), calls=%async_computation.1 | async-start | bytes 8388608
  111.8 7.2 %slice-start.1 = ((s8[4608000]{0:T(1024)(128)(4,1)}), s8[413696]{0:T(1024)(128)(4,1)S(1)}, s32[]{:S(2)}) async-start(s8[4608000]{0:T(1024)(128)(4,1)} %bitcast.81), calls=%async_computation.2 | async-start | bytes 827392
  127.8 2.2 copy-start.1
  135.2 105.8 %all-to-all-start = ((f32[384,4,3,256]{3,1,2,0:T(4,128)}), f32[384,4,3,256]{3,1,2,0:T(4,128)}, u32[]{:S(2)}, u32[]{:S(2)}) async-start(f32[384,4,3,256]{3,1,2,0:T(4,128)} %copy.29), calls=%async_computation | async-start | bytes 9437184 | tf_op jit(solution)/shard_map/all_to_all | solution.py:123
  258.4 1.2 copy-start.2
where the time goes:
time: 263 us; the launch traced here: 260 us
  blocking collectives  106 us (40%)
  waiting for transfers between devices  97.3 us (37%)
  local copies, waits for them, and re-layouts  26.4 us (10%)
  other arithmetic  16 us (6%)
  matrix products  8.73 us (3%)
  starting transfers between devices  4.78 us (2%)
    all_to_all x1, waiting for transfers between devices, local(): lax.all_to_all(stress, 'freq', split_axis=0, concat_axis=3, tiled=True)  97.3 us
    psum x1, blocking collectives, local(): wheel_rows = lax.psum(picked, ('elem', 'freq'))  81.6 us
    all_gather x1, blocking collectives, local(): factors = lax.all_gather(own_factors, 'freq', axis=1, tiled=True)  24 us
    all_to_all x2, local copies, waits for them, and re-layouts, local(): lax.all_to_all(stress, 'freq', split_axis=0, concat_axis=3, tiled=True)  13.2 us
    dot_general x1, matrix products, local(): jnp.einsum('fkm,cme->fkce', modal, stress_modes, preferred_element_type=j...  8.73 us
    another operation x1, other arithmetic  7.14 us
  transfers between devices with their start and end apart: 1, of which 1 were waited for; matrix products, arithmetic and copies ran while one was open for 1% of the time, Pallas kernels for 0%

commit v1 on v0

v1 whole, which is shorter than its diff:
```python
import functools
import math

import jax
import jax.numpy as jnp
from jax import lax
from jax.experimental import pallas as pl
from jax.experimental.pallas import tpu as pltpu
from jax.sharding import PartitionSpec as P

NBINS = 4096
PHASES = 64
LANES = 128
PEERS = 16
MESH = pl.DeviceIdType.MESH


def partner(freq, step):
    across = 1 - step % 2
    rank = step // 2
    odd = rank % 2
    along = odd * (4 - (rank + 1) // 2) + (1 - odd) * (4 + rank // 2)
    x_lo, z = freq // 8, freq % 8
    return ((x_lo + across) % 2) * 8 + (z + along) % 8


def source(freq, step):
    across = 1 - step % 2
    rank = step // 2
    odd = rank % 2
    along = odd * (4 - (rank + 1) // 2) + (1 - odd) * (4 + rank // 2)
    x_lo, z = freq // 8, freq % 8
    return ((x_lo + across) % 2) * 8 + (z + 8 - along) % 8


def kernel(
    modes_any,
    shapes_any,
    nodes_any,
    natural_any,
    damping_any,
    bins_any,
    phase_any,
    road_any,
    block_any,
    scale_any,
    spectra_ref,
    moments_ref,
    modes,
    shapes,
    nodes,
    natural,
    damping,
    bins,
    phase,
    road,
    block,
    scale,
    picked,
    partial,
    summed,
    wheels,
    factors,
    scaling,
    modal,
    outgoing,
    arrived,
    spread,
    load_sem,
    send_a,
    recv_a,
    send_b,
    recv_b,
    send_c,
    recv_c,
    send_f,
    recv_f,
    send_s,
    recv_s,
):
    elem = lax.axis_index("elem")
    freq = lax.axis_index("freq")
    num_modes = natural.shape[1]
    lines = bins.shape[1]
    width = block.shape[1]
    tiles = -(-num_modes // LANES)
    rows_here = shapes.shape[0]

    barrier = pltpu.get_barrier_semaphore()

    def greet(step, carry):
        pl.semaphore_signal(barrier, inc=1, device_id=(elem, (freq + step) % PEERS), device_id_type=MESH)
        pl.semaphore_signal(barrier, inc=1, device_id=((elem + step) % PEERS, freq), device_id_type=MESH)
        return carry

    lax.fori_loop(1, PEERS, greet, 0)

    pairs = (
        (shapes_any, shapes),
        (nodes_any, nodes),
        (bins_any, bins),
        (phase_any, phase),
        (road_any, road),
        (natural_any, natural),
        (damping_any, damping),
        (block_any, block),
        (scale_any, scale),
        (modes_any, modes),
    )
    loads = [pltpu.make_async_copy(a, b, load_sem.at[i]) for i, (a, b) in enumerate(pairs)]
    for load in loads:
        load.start()
    for load in loads[:9]:
        load.wait()

    first_row = (elem * PEERS + freq) * rows_here
    row_number = lax.broadcasted_iota(jnp.int32, (rows_here, LANES), 0) + first_row
    masks = [row_number == nodes[:, w : w + 1] for w in range(4)]
    for t in range(tiles):
        lo, hi = t * LANES, min((t + 1) * LANES, num_modes)
        piece = shapes[:, lo:hi]
        found = [
            jnp.sum(jnp.where(m[:, : hi - lo], piece, 0.0), axis=0, keepdims=True) for m in masks
        ]
        picked[t // 2, (t % 2) * 4 : (t % 2) * 4 + 4, : hi - lo] = jnp.concatenate(found, axis=0)
    for j in range((tiles + 1) // 2, PEERS):
        picked[j] = jnp.zeros((8, LANES), jnp.float32)

    ratio = bins[...].astype(jnp.float32) / NBINS
    angle = 2.0 * math.pi / PHASES * phase[...].astype(jnp.float32)
    root = jnp.sqrt(road[...])
    amplitude = jnp.concatenate([root[0:1], root[0:1], root[1:2], root[1:2]], axis=0)
    table = jnp.concatenate(
        [
            ratio,
            amplitude * jnp.cos(angle),
            amplitude * jnp.sin(angle),
            jnp.zeros((LANES - 9, lines), jnp.float32),
        ],
        axis=0,
    )
    table = jnp.concatenate([table, jnp.zeros((LANES, LANES - lines), jnp.float32)], axis=1)
    factors[freq] = jnp.transpose(table)[:lines]

    pl.semaphore_wait(barrier, 2 * (PEERS - 1))

    def copy_a(step):
        peer = (elem + step) % PEERS
        return pltpu.make_async_remote_copy(
            src_ref=picked.at[peer],
            dst_ref=partial.at[step],
            send_sem=send_a.at[step],
            recv_sem=recv_a.at[step],
            device_id=(peer, freq),
            device_id_type=MESH,
        )

    def copy_f(step):
        return pltpu.make_async_remote_copy(
            src_ref=factors.at[freq],
            dst_ref=factors.at[freq],
            send_sem=send_f.at[step],
            recv_sem=recv_f.at[step],
            device_id=(elem, partner(freq, step)),
            device_id_type=MESH,
        )

    def copy_b(step):
        return pltpu.make_async_remote_copy(
            src_ref=summed.at[PEERS - 1],
            dst_ref=summed.at[step],
            send_sem=send_b.at[step],
            recv_sem=recv_b.at[step],
            device_id=(elem, partner(freq, step)),
            device_id_type=MESH,
        )

    def copy_c(step):
        return pltpu.make_async_remote_copy(
            src_ref=wheels.at[elem],
            dst_ref=wheels.at[elem],
            send_sem=send_c.at[step],
            recv_sem=recv_c.at[step],
            device_id=((elem + step) % PEERS, freq),
            device_id_type=MESH,
        )

    def started(copy, low, high):
        def body(step, carry):
            copy(step).start()
            return carry

        lax.fori_loop(low, high, body, 0)

    def received(copy, low, high):
        def body(step, carry):
            copy(step).wait_recv()
            return carry

        lax.fori_loop(low, high, body, 0)

    def sent(copy, low, high):
        def body(step, carry):
            copy(step).wait_send()
            return carry

        lax.fori_loop(low, high, body, 0)

    started(copy_a, 1, PEERS)
    started(copy_f, 0, PEERS - 1)
    partial[0] = picked[elem]

    sets = block[...]
    found = jnp.zeros(sets.shape, jnp.float32)
    for i in range(scale.shape[1]):
        found = jnp.where(sets == i, scale[:, i : i + 1], found)
    scaling[...] = found
    moments_ref[...] = jnp.zeros(moments_ref.shape, jnp.float32)

    received(copy_a, 1, PEERS)
    summed[PEERS - 1] = jnp.sum(partial[...], axis=0)
    started(copy_b, 0, PEERS - 1)
    received(copy_b, 0, PEERS - 1)
    wheels[elem] = jnp.sum(summed[...], axis=0)
    started(copy_c, 1, PEERS)
    loads[9].wait()
    received(copy_f, 0, PEERS - 1)
    received(copy_c, 1, PEERS)

    def copy_s(step):
        return pltpu.make_async_remote_copy(
            src_ref=outgoing.at[step],
            dst_ref=arrived.at[step],
            send_sem=send_s.at[step],
            recv_sem=recv_s.at[step],
            device_id=(elem, partner(freq, step)),
            device_id_type=MESH,
        )

    def serve(step, carry):
        table = factors[partner(freq, step)]
        column = [jnp.broadcast_to(table[:, i : i + 1], (lines, LANES)) for i in range(9)]
        square = column[0] * column[0]
        for t in range(tiles):
            lo, hi = t * LANES, min((t + 1) * LANES, num_modes)
            size = hi - lo
            v = natural[:, lo:hi]
            z = damping[:, lo:hi]
            w = [wheels[t // 2, (t % 2) * 4 + i : (t % 2) * 4 + i + 1, :size] for i in range(4)]
            col = [c[:, :size] for c in column]
            own = v * v
            detune = own - square[:, :size]
            damped = (2.0 * z * v) * col[0]
            gain = own / (detune * detune + damped * damped)
            gain_real = gain * detune
            gain_imag = gain * damped
            for k in range(2):
                real = col[1 + 2 * k] * w[2 * k] + col[2 + 2 * k] * w[2 * k + 1]
                imag = col[5 + 2 * k] * w[2 * k] + col[6 + 2 * k] * w[2 * k + 1]
                both = jnp.concatenate(
                    [
                        gain_real * real - gain_imag * imag,
                        -(gain_real * imag + gain_imag * real),
                    ],
                    axis=0,
                )
                modal[2 * k * lines : 2 * (k + 1) * lines, lo:hi] = both.astype(jnp.bfloat16)
        factor = scaling[...]
        stress = []
        for c in range(3):
            product = jnp.dot(modal[...], modes[c], preferred_element_type=jnp.float32) * factor
            stress.append([product[k * lines : (k + 1) * lines] for k in range(4)])

        def real_of(a, b):
            a, b = stress[a], stress[b]
            return a[0] * b[0] + a[1] * b[1] + (a[2] * b[2] + a[3] * b[3])

        def imag_of(a, b):
            a, b = stress[a], stress[b]
            return a[1] * b[0] - a[0] * b[1] + (a[3] * b[2] - a[2] * b[3])

        cross = [
            real_of(0, 0),
            real_of(1, 1),
            real_of(2, 2),
            real_of(0, 1),
            real_of(0, 2),
            real_of(1, 2),
            imag_of(0, 1),
            imag_of(0, 2),
            imag_of(1, 2),
        ]
        for i, value in enumerate(cross):
            halves = jnp.concatenate([value[:, :LANES], value[:, LANES:]], axis=0)
            outgoing[step, i] = halves.astype(jnp.bfloat16)

        @pl.when(step < PEERS - 1)
        def _():
            copy_s(step).start()

        equivalent = cross[0] + cross[1] - cross[3] + 3.0 * cross[2]
        r = table[:, 0:1]
        r2 = r * r
        listed = [
            jnp.sum(value, axis=0, keepdims=True)
            for value in (equivalent, r * equivalent, r2 * equivalent, (r2 * r2) * equivalent)
        ]
        moments_ref[...] += jnp.concatenate(listed, axis=0)
        return carry

    lax.fori_loop(0, PEERS, serve, 0)
    moments_ref[...] = moments_ref[...] / (PEERS * lines)

    def place(ref, step):
        start = source(freq, step) * width
        for half in range(2):
            for i in range(9):
                value = ref[i, half * lines : (half + 1) * lines].astype(jnp.float32)
                spread[half, pl.ds(i, lines, stride=16), :] = value
            at = pl.multiple_of(start + half * LANES, LANES)
            for f in range(lines):
                spectra_ref[f, :, pl.ds(at, LANES)] = spread[half, f * 16 : f * 16 + 9, :].astype(
                    jnp.bfloat16
                )

    place(outgoing.at[PEERS - 1], PEERS - 1)

    def take(step, carry):
        copy_s(step).wait_recv()
        place(arrived.at[step], step)
        return carry

    lax.fori_loop(0, PEERS - 1, take, 0)
    sent(copy_a, 1, PEERS)
    sent(copy_f, 0, PEERS - 1)
    sent(copy_b, 0, PEERS - 1)
    sent(copy_c, 1, PEERS)
    sent(copy_s, 0, PEERS - 1)


def local(*args):
    modes, shapes, nodes, natural, damping, bins, phase, road, block, scale = args
    row = [a.reshape(1, -1) for a in (nodes, natural, damping, bins)]
    args = (modes, shapes, *row, phase, road, block.reshape(1, -1), scale.reshape(1, -1))
    num_modes, width = modes.shape[1:]
    lines = bins.shape[0]
    f32, bf16 = jnp.float32, jnp.bfloat16
    sems = pltpu.SemaphoreType.DMA((PEERS,))
    return pl.pallas_call(
        kernel,
        out_shape=(
            jax.ShapeDtypeStruct((lines, 9, PEERS * width), bf16),
            jax.ShapeDtypeStruct((4, width), f32),
        ),
        in_specs=[pl.BlockSpec(memory_space=pl.ANY)] * len(args),
        out_specs=(pl.BlockSpec(memory_space=pltpu.VMEM),) * 2,
        scratch_shapes=[
            *[pltpu.VMEM(a.shape, a.dtype) for a in args],
            pltpu.VMEM((PEERS, 8, LANES), f32),
            pltpu.VMEM((PEERS, 8, LANES), f32),
            pltpu.VMEM((PEERS, 8, LANES), f32),
            pltpu.VMEM((PEERS, 8, LANES), f32),
            pltpu.VMEM((PEERS, lines, LANES), f32),
            pltpu.VMEM((1, width), f32),
            pltpu.VMEM((4 * lines, num_modes), bf16),
            pltpu.VMEM((PEERS, 9, 2 * lines, LANES), bf16),
            pltpu.VMEM((PEERS, 9, 2 * lines, LANES), bf16),
            pltpu.VMEM((2, 16 * lines, LANES), f32),
            sems,
            *[sems] * 10,
        ],
        compiler_params=pltpu.CompilerParams(
            collective_id=0, has_side_effects=True, vmem_limit_bytes=40 << 20
        ),
        cost_estimate=pl.CostEstimate(flops=7_100_000_000, bytes_accessed=10_000_000, transcendentals=0),
    )(*args)


def solution(mesh):
    placed = (
        P(None, None, ("elem", "freq")),
        P(("elem", "freq"), None),
        P(),
        P(),
        P(),
        P("freq"),
        P(None, "freq"),
        P(None, "freq"),
        P(("elem", "freq")),
        P(),
    )
    return jax.shard_map(
        local,
        mesh=mesh,
        in_specs=placed,
        out_specs=(P("freq", None, "elem"), P(None, ("elem", "freq"))),
        check_vma=False,
    )
```

time: 263 us -> 82.5 us (0.31); the launches traced: 260 us -> 82.2 us
  blocking collectives: 106 us -> 0 us
  waiting for transfers between devices: 97.3 us -> 0 us
  Pallas kernels: 0 us -> 70 us
  other arithmetic: 16 us -> 0 us
  local copies, waits for them, and re-layouts: 26.4 us -> 11.5 us
  matrix products: 8.73 us -> 0 us
  starting transfers between devices: 4.78 us -> 0 us
    all_to_all x1 -> x0, waiting for transfers between devices: 97.3 us -> none  [local(): lax.all_to_all(stress, 'freq', split_axis=0, concat_axis=3, tiled=True)]
    psum x1 -> x0, blocking collectives: 81.6 us -> none  [local(): wheel_rows = lax.psum(picked, ('elem', 'freq'))]
    pallas_call x0 -> x1, Pallas kernels: none -> 70 us  [local(): pl.pallas_call(kernel, out_shape=(jax.ShapeDtypeStruct((lines, 9, PEERS *...]
    all_gather x1 -> x0, blocking collectives: 24 us -> none  [local(): factors = lax.all_gather(own_factors, 'freq', axis=1, tiled=True)]
    all_to_all x2 -> x0, local copies, waits for them, and re-layouts: 13.2 us -> none  [local(): lax.all_to_all(stress, 'freq', split_axis=0, concat_axis=3, tiled=True)]
    dot_general x1 -> x0, matrix products: 8.73 us -> none  [local(): jnp.einsum('fkm,cme->fkce', modal, stress_modes, preferred_element_type=j...]
    another operation x2 -> x0, other arithmetic: 7.74 us -> none
    unnamed x19 -> x21, local copies, waits for them, and re-layouts: 3.67 us -> 9.23 us
  transfers between devices with their start and end apart: 1 -> 0, of which waited for: 1 -> 0; matrix products, arithmetic and copies ran while one was open for 1% -> 0% of each run, Pallas kernels for 0% -> 0%
where the time goes in v1:
time: 82.5 us; the launch traced here: 82.2 us
  Pallas kernels  70 us (85%)
  local copies, waits for them, and re-layouts  11.5 us (14%)
    pallas_call x1, Pallas kernels, local(): pl.pallas_call(kernel, out_shape=(jax.ShapeDtypeStruct((lines, 9, PEERS *...  70 us
    unnamed x21, local copies, waits for them, and re-layouts  9.23 us
    pallas_call x1, local copies, waits for them, and re-layouts, local(): pl.pallas_call(kernel, out_shape=(jax.ShapeDtypeStruct((lines, 9, PEERS *...  2.28 us

profile of v1, /device:TPU:1, one launch (start us, length us, event | category | flops | bytes accessed | tf_op | source)
XLA Modules:
  0.0 82.2 jit_solution(13570807617826541011)
XLA Ops:
  0.6 0.0 copy-start
  0.6 2.3 %copy-done = bf16[3,3000,256]{2,1,0:T(8,128)(2,1)S(1)} copy-done((bf16[3,3000,256]{2,1,0:T(8,128)(2,1)S(1)}, bf16[3,3000,256]{2,1,0:T(8,128)(2,1)}, u32[]{:S(2)}) %copy-start) | copy-done | bytes 4608024
  2.9 0.0 copy-start.1
  2.9 0.9 %copy-done.1 = f32[16,3000]{1,0:T(8,128)S(1)} copy-done((f32[16,3000]{1,0:T(8,128)S(1)}, f32[16,3000]{1,0:T(8,128)}, u32[]{:S(2)}) %copy-start.1) | copy-done | bytes 192024
  3.9 0.0 copy-start.2
  3.9 0.7 copy-done.2
  4.6 0.0 copy-start.3
  4.6 0.7 copy-done.3
  5.3 0.0 copy-start.4
  5.3 0.7 copy-done.4
  6.0 0.0 copy-start.5
  6.0 0.7 copy-done.5
  6.6 0.0 copy-start.6
  6.6 0.7 copy-done.6
  7.3 0.0 copy-start.7
  7.3 0.7 copy-done.7
  8.0 0.0 copy-start.8
  8.0 0.7 copy-done.8
  8.6 0.0 copy-start.9
  8.6 0.7 copy-done.9
  9.3 70.0 %shard_map.113 = (bf16[24,9,4096]{2,1,0:T(8,128)(2,1)S(1)}, f32[4,256]{1,0:T(4,128)S(1)}) custom-call(bf16[3,3000,256]{2,1,0:T(8,128)(2,1)S(1)} %copy-done, f32[16,3000]{1,0:T(8,128)S(1)} %copy-done.1, s32[1,4]{1,0:T(1,128)S(1)} %bitcast.9, f32[1,3000]{1,0:T(1,128)S(1)} %bitcast.6, f32[1,3000]{1,0:T(1,128)S(1)} %bitcast.7, s32[1,24]{1,0:T(1,128)S(1)} %bitcast.10, ...), custom_call_target="tpu_custom_call" | custom-call | flops 7100000256 | bytes 10000000 | tf_op jit(solution)/shard_map/pallas_call | solution.py:349
  79.3 2.3 %copy.12 = bf16[24,9,4096]{2,0,1:T(8,128)(2,1)} copy(bf16[24,9,4096]{2,1,0:T(8,128)(2,1)S(1)} %get-tuple-element.2) | data formatting | bytes 3538944 | tf_op jit(solution)/shard_map/pallas_call | solution.py:349
  81.6 0.6 copy.14
Async XLA Ops:
  0.6 2.3 %copy-start = (bf16[3,3000,256]{2,1,0:T(8,128)(2,1)S(1)}, bf16[3,3000,256]{2,1,0:T(8,128)(2,1)}, u32[]{:S(2)}) copy-start(bf16[3,3000,256]{2,1,0:T(8,128)(2,1)} %modes_any.1) | copy-start | bytes 13824004
  2.9 0.9 %copy-start.1 = (f32[16,3000]{1,0:T(8,128)S(1)}, f32[16,3000]{1,0:T(8,128)}, u32[]{:S(2)}) copy-start(f32[16,3000]{1,0:T(8,128)} %shapes_any.1) | copy-start | bytes 576004
  3.9 0.7 copy-start.2
  4.6 0.7 copy-start.3
  5.3 0.7 copy-start.4
  6.0 0.7 copy-start.5
  6.6 0.7 copy-start.6
  7.3 0.7 copy-start.7
  8.0 0.7 copy-start.8
  8.6 0.7 copy-start.9

commit v2 on v1

--- a/solution.py
+++ b/solution.py
@@ -24,13 +24,13 @@
     return ((x_lo + across) % 2) * 8 + (z + along) % 8
 
 
-def source(freq, step):
-    across = 1 - step % 2
-    rank = step // 2
-    odd = rank % 2
-    along = odd * (4 - (rank + 1) // 2) + (1 - odd) * (4 + rank // 2)
-    x_lo, z = freq // 8, freq % 8
-    return ((x_lo + across) % 2) * 8 + (z + 8 - along) % 8
+ELEM_STEPS = [(x, y, c) for y in (2, 1, 3, 0) for x in (1, 0) for c in (1, 0)][:-1]
+
+
+def elem_peer(elem, step):
+    x, y, c = ELEM_STEPS[step]
+    x_hi, y_at, core = elem // 8, (elem // 2) % 4, elem % 2
+    return ((x_hi + x) % 2) * 8 + ((y_at + y) % 4) * 2 + (core + c) % 2
 
 
 def kernel(
@@ -64,8 +64,6 @@
     scaling,
     modal,
     outgoing,
-    arrived,
-    spread,
     load_sem,
     send_a,
     recv_a,
@@ -88,12 +86,9 @@
 
     barrier = pltpu.get_barrier_semaphore()
 
-    def greet(step, carry):
-        pl.semaphore_signal(barrier, inc=1, device_id=(elem, (freq + step) % PEERS), device_id_type=MESH)
-        pl.semaphore_signal(barrier, inc=1, device_id=((elem + step) % PEERS, freq), device_id_type=MESH)
-        return carry
-
-    lax.fori_loop(1, PEERS, greet, 0)
+    for step in range(PEERS - 1):
+        for peer in ((elem, partner(freq, step)), (elem_peer(elem, step), freq)):
+            pl.semaphore_signal(barrier, inc=1, device_id=peer, device_id_type=MESH)
 
     pairs = (
         (shapes_any, shapes),
@@ -145,7 +140,7 @@
     pl.semaphore_wait(barrier, 2 * (PEERS - 1))
 
     def copy_a(step):
-        peer = (elem + step) % PEERS
+        peer = elem_peer(elem, step)
         return pltpu.make_async_remote_copy(
             src_ref=picked.at[peer],
             dst_ref=partial.at[step],
@@ -181,34 +176,25 @@
             dst_ref=wheels.at[elem],
             send_sem=send_c.at[step],
             recv_sem=recv_c.at[step],
-            device_id=((elem + step) % PEERS, freq),
-            device_id_type=MESH,
-        )
-
-    def started(copy, low, high):
-        def body(step, carry):
+            device_id=(elem_peer(elem, step), freq),
+            device_id_type=MESH,
+        )
+
+    def started(copy):
+        for step in range(PEERS - 1):
             copy(step).start()
-            return carry
-
-        lax.fori_loop(low, high, body, 0)
-
-    def received(copy, low, high):
-        def body(step, carry):
+
+    def received(copy):
+        for step in range(PEERS - 1):
             copy(step).wait_recv()
-            return carry
-
-        lax.fori_loop(low, high, body, 0)
-
-    def sent(copy, low, high):
-        def body(step, carry):
+
+    def sent(copy):
+        for step in range(PEERS - 1):
             copy(step).wait_send()
-            return carry
-
-        lax.fori_loop(low, high, body, 0)
-
-    started(copy_a, 1, PEERS)
-    started(copy_f, 0, PEERS - 1)
-    partial[0] = picked[elem]
+
+    started(copy_a)
+    started(copy_f)
+    partial[PEERS - 1] = picked[elem]
 
     sets = block[...]
     found = jnp.zeros(sets.shape, jnp.float32)
@@ -217,20 +203,22 @@
     scaling[...] = found
     moments_ref[...] = jnp.zeros(moments_ref.shape, jnp.float32)
 
-    received(copy_a, 1, PEERS)
+    received(copy_a)
     summed[PEERS - 1] = jnp.sum(partial[...], axis=0)
-    started(copy_b, 0, PEERS - 1)
-    received(copy_b, 0, PEERS - 1)
+    started(copy_b)
+    received(copy_b)
     wheels[elem] = jnp.sum(summed[...], axis=0)
-    started(copy_c, 1, PEERS)
+    started(copy_c)
     loads[9].wait()
-    received(copy_f, 0, PEERS - 1)
-    received(copy_c, 1, PEERS)
+    received(copy_f)
+    received(copy_c)
+
+    here = pl.ds(pl.multiple_of(freq * width, width), width)
 
     def copy_s(step):
         return pltpu.make_async_remote_copy(
             src_ref=outgoing.at[step],
-            dst_ref=arrived.at[step],
+            dst_ref=spectra_ref.at[:, :, here],
             send_sem=send_s.at[step],
             recv_sem=recv_s.at[step],
             device_id=(elem, partner(freq, step)),
@@ -291,8 +279,7 @@
             imag_of(1, 2),
         ]
         for i, value in enumerate(cross):
-            halves = jnp.concatenate([value[:, :LANES], value[:, LANES:]], axis=0)
-            outgoing[step, i] = halves.astype(jnp.bfloat16)
+            outgoing[step, i] = value.astype(jnp.bfloat16)
 
         @pl.when(step < PEERS - 1)
         def _():
@@ -311,48 +298,31 @@
     lax.fori_loop(0, PEERS, serve, 0)
     moments_ref[...] = moments_ref[...] / (PEERS * lines)
 
-    def place(ref, step):
-        start = source(freq, step) * width
-        for half in range(2):
-            for i in range(9):
-                value = ref[i, half * lines : (half + 1) * lines].astype(jnp.float32)
-                spread[half, pl.ds(i, lines, stride=16), :] = value
-            at = pl.multiple_of(start + half * LANES, LANES)
-            for f in range(lines):
-                spectra_ref[f, :, pl.ds(at, LANES)] = spread[half, f * 16 : f * 16 + 9, :].astype(
-                    jnp.bfloat16
-                )
-
-    place(outgoing.at[PEERS - 1], PEERS - 1)
-
-    def take(step, carry):
+    keep = pltpu.make_async_copy(outgoing.at[PEERS - 1], spectra_ref.at[:, :, here], load_sem.at[0])
+    keep.start()
+    for step in range(PEERS - 1):
         copy_s(step).wait_recv()
-        place(arrived.at[step], step)
-        return carry
-
-    lax.fori_loop(0, PEERS - 1, take, 0)
-    sent(copy_a, 1, PEERS)
-    sent(copy_f, 0, PEERS - 1)
-    sent(copy_b, 0, PEERS - 1)
-    sent(copy_c, 1, PEERS)
-    sent(copy_s, 0, PEERS - 1)
+    keep.wait()
+    for copy in (copy_a, copy_f, copy_b, copy_c, copy_s):
+        sent(copy)
 
 
 def local(*args):
     modes, shapes, nodes, natural, damping, bins, phase, road, block, scale = args
     row = [a.reshape(1, -1) for a in (nodes, natural, damping, bins)]
     args = (modes, shapes, *row, phase, road, block.reshape(1, -1), scale.reshape(1, -1))
+    args = [pltpu.with_memory_space_constraint(a, pltpu.HBM) for a in args]
     num_modes, width = modes.shape[1:]
     lines = bins.shape[0]
     f32, bf16 = jnp.float32, jnp.bfloat16
     sems = pltpu.SemaphoreType.DMA((PEERS,))
-    return pl.pallas_call(
+    spectra, moments = pl.pallas_call(
         kernel,
         out_shape=(
-            jax.ShapeDtypeStruct((lines, 9, PEERS * width), bf16),
+            jax.ShapeDtypeStruct((9, lines, PEERS * width), bf16),
             jax.ShapeDtypeStruct((4, width), f32),
         ),
-        in_specs=[pl.BlockSpec(memory_space=pl.ANY)] * len(args),
+        in_specs=[pl.BlockSpec(memory_space=pltpu.HBM)] * len(args),
         out_specs=(pl.BlockSpec(memory_space=pltpu.VMEM),) * 2,
         scratch_shapes=[
             *[pltpu.VMEM(a.shape, a.dtype) for a in args],
@@ -363,9 +333,7 @@
             pltpu.VMEM((PEERS, lines, LANES), f32),
             pltpu.VMEM((1, width), f32),
             pltpu.VMEM((4 * lines, num_modes), bf16),
-            pltpu.VMEM((PEERS, 9, 2 * lines, LANES), bf16),
-            pltpu.VMEM((PEERS, 9, 2 * lines, LANES), bf16),
-            pltpu.VMEM((2, 16 * lines, LANES), f32),
+            pltpu.VMEM((PEERS, 9, lines, width), bf16),
             sems,
             *[sems] * 10,
         ],
@@ -374,6 +342,7 @@
         ),
         cost_estimate=pl.CostEstimate(flops=7_100_000_000, bytes_accessed=10_000_000, transcendentals=0),
     )(*args)
+    return jnp.transpose(spectra, (1, 0, 2)), moments
 
 
 def solution(mesh):

time: 82.5 us -> 71.1 us (0.86)
  local copies, waits for them, and re-layouts: 11.5 us -> 1.8 us
  Pallas kernels: 70 us -> 68.6 us
    unnamed x21 -> x2, local copies, waits for them, and re-layouts: 9.23 us -> 1.8 us
    pallas_call x1 -> x0, local copies, waits for them, and re-layouts: 2.28 us -> none  [local(): pl.pallas_call(kernel, out_shape=(jax.ShapeDtypeStruct((lines, 9, PEERS *...]
    pallas_call x1, Pallas kernels: 70 us -> 68.6 us  [local(): pl.pallas_call(kernel, out_shape=(jax.ShapeDtypeStruct((9, lines, PEERS *...]
where the time goes in v2:
time: 71.1 us; the launch traced here: 71 us
  Pallas kernels  68.6 us (96%)
  local copies, waits for them, and re-layouts  1.8 us (3%)
    pallas_call x1, Pallas kernels, local(): pl.pallas_call(kernel, out_shape=(jax.ShapeDtypeStruct((9, lines, PEERS *...  68.6 us
    unnamed x2, local copies, waits for them, and re-layouts  1.8 us

profile of v2, /device:TPU:1, one launch (start us, length us, event | category | flops | bytes accessed | tf_op | source)
XLA Modules:
  0.0 71.0 jit_solution(12380365351810225874)
XLA Ops:
  0.6 68.6 %shard_map.113 = (bf16[9,24,4096]{2,1,0:T(8,128)(2,1)S(1)}, f32[4,256]{1,0:T(4,128)S(1)}) custom-call(bf16[3,3000,256]{2,1,0:T(8,128)(2,1)} %modes_any.1, f32[16,3000]{1,0:T(8,128)} %shapes_any.1, s32[1,4]{1,0:T(1,128)} %bitcast.11, f32[1,3000]{1,0:T(1,128)} %bitcast.8, f32[1,3000]{1,0:T(1,128)} %bitcast.9, s32[1,24]{1,0:T(1,128)} %bitcast.12, ...), custom_call_target="tpu_custom_call" | custom-call | flops 7100000256 | bytes 10000000 | tf_op jit(solution)/shard_map/pallas_call | solution.py:319
  69.2 1.2 %copy.14 = bf16[24,9,4096]{2,0,1:T(8,128)(2,1)} copy(bf16[24,9,4096]{2,0,1:T(8,128)(2,1)S(1)} %bitcast.7) | data formatting | bytes 3538944
  70.5 0.6 copy.15

commit v3 on v2

--- a/solution.py
+++ b/solution.py
@@ -22,6 +22,29 @@
     along = odd * (4 - (rank + 1) // 2) + (1 - odd) * (4 + rank // 2)
     x_lo, z = freq // 8, freq % 8
     return ((x_lo + across) % 2) * 8 + (z + along) % 8
+
+
+def source(freq, step):
+    across = 1 - step % 2
+    rank = step // 2
+    odd = rank % 2
+    along = odd * (4 - (rank + 1) // 2) + (1 - odd) * (4 + rank // 2)
+    x_lo, z = freq // 8, freq % 8
+    return ((x_lo + across) % 2) * 8 + (z + 8 - along) % 8
+
+
+def unit(parts):
+    top = jnp.abs(parts[0])
+    for part in parts[1:]:
+        top = jnp.maximum(top, jnp.abs(part))
+    some = top > 1e-37
+    scaled = [part * (1.0 / jnp.where(some, top, 1.0)) for part in parts]
+    total = scaled[0] * scaled[0]
+    for part in scaled[1:]:
+        total += part * part
+    shrink = lax.rsqrt(jnp.where(some, total, 1.0))
+    direction = [jnp.where(some, part * shrink, 1.0 if i == 0 else 0.0) for i, part in enumerate(scaled)]
+    return direction, jnp.where(some, top * (total * shrink), 0.0)
 
 
 ELEM_STEPS = [(x, y, c) for y in (2, 1, 3, 0) for x in (1, 0) for c in (1, 0)][:-1]
@@ -64,6 +87,7 @@
     scaling,
     modal,
     outgoing,
+    arrived,
     load_sem,
     send_a,
     recv_a,
@@ -71,8 +95,6 @@
     recv_b,
     send_c,
     recv_c,
-    send_f,
-    recv_f,
     send_s,
     recv_s,
 ):
@@ -125,17 +147,10 @@
     angle = 2.0 * math.pi / PHASES * phase[...].astype(jnp.float32)
     root = jnp.sqrt(road[...])
     amplitude = jnp.concatenate([root[0:1], root[0:1], root[1:2], root[1:2]], axis=0)
-    table = jnp.concatenate(
-        [
-            ratio,
-            amplitude * jnp.cos(angle),
-            amplitude * jnp.sin(angle),
-            jnp.zeros((LANES - 9, lines), jnp.float32),
-        ],
-        axis=0,
-    )
-    table = jnp.concatenate([table, jnp.zeros((LANES, LANES - lines), jnp.float32)], axis=1)
-    factors[freq] = jnp.transpose(table)[:lines]
+    waves = jnp.concatenate([amplitude * jnp.cos(angle), amplitude * jnp.sin(angle)], axis=0)
+    ratios = jnp.concatenate([ratio, jnp.zeros((7, lines), jnp.float32)], axis=0)
+    rest = jnp.zeros((8, LANES - 2 * lines), jnp.float32)
+    summed[PEERS - 1, 8:] = jnp.concatenate([waves, ratios, rest], axis=1)
 
     pl.semaphore_wait(barrier, 2 * (PEERS - 1))
 
@@ -150,16 +165,6 @@
             device_id_type=MESH,
         )
 
-    def copy_f(step):
-        return pltpu.make_async_remote_copy(
-            src_ref=factors.at[freq],
-            dst_ref=factors.at[freq],
-            send_sem=send_f.at[step],
-            recv_sem=recv_f.at[step],
-            device_id=(elem, partner(freq, step)),
-            device_id_type=MESH,
-        )
-
     def copy_b(step):
         return pltpu.make_async_remote_copy(
             src_ref=summed.at[PEERS - 1],
@@ -193,7 +198,6 @@
             copy(step).wait_send()
 
     started(copy_a)
-    started(copy_f)
     partial[PEERS - 1] = picked[elem]
 
     sets = block[...]
@@ -204,21 +208,20 @@
     moments_ref[...] = jnp.zeros(moments_ref.shape, jnp.float32)
 
     received(copy_a)
-    summed[PEERS - 1] = jnp.sum(partial[...], axis=0)
+    summed[PEERS - 1, :8] = jnp.sum(partial[...], axis=0)
     started(copy_b)
     received(copy_b)
-    wheels[elem] = jnp.sum(summed[...], axis=0)
+    wheels[elem] = jnp.sum(summed[:, :8], axis=0)
     started(copy_c)
+    for step in range(PEERS):
+        factors[source(freq, step)] = jnp.transpose(summed[step, 8:])[: 2 * lines]
     loads[9].wait()
-    received(copy_f)
     received(copy_c)
-
-    here = pl.ds(pl.multiple_of(freq * width, width), width)
 
     def copy_s(step):
         return pltpu.make_async_remote_copy(
             src_ref=outgoing.at[step],
-            dst_ref=spectra_ref.at[:, :, here],
+            dst_ref=arrived.at[step],
             send_sem=send_s.at[step],
             recv_sem=recv_s.at[step],
             device_id=(elem, partner(freq, step)),
@@ -227,7 +230,9 @@
 
     def serve(step, carry):
         table = factors[partner(freq, step)]
-        column = [jnp.broadcast_to(table[:, i : i + 1], (lines, LANES)) for i in range(9)]
+        r = table[lines:, 0:1]
+        column = [r] + [table[:lines, i : i + 1] for i in range(8)]
+        column = [jnp.broadcast_to(c, (lines, LANES)) for c in column]
         square = column[0] * column[0]
         for t in range(tiles):
             lo, hi = t * LANES, min((t + 1) * LANES, num_modes)
@@ -260,33 +265,44 @@
             stress.append([product[k * lines : (k + 1) * lines] for k in range(4)])
 
         def real_of(a, b):
-            a, b = stress[a], stress[b]
             return a[0] * b[0] + a[1] * b[1] + (a[2] * b[2] + a[3] * b[3])
 
         def imag_of(a, b):
-            a, b = stress[a], stress[b]
             return a[1] * b[0] - a[0] * b[1] + (a[3] * b[2] - a[2] * b[3])
 
-        cross = [
-            real_of(0, 0),
-            real_of(1, 1),
-            real_of(2, 2),
-            real_of(0, 1),
-            real_of(0, 2),
-            real_of(1, 2),
-            imag_of(0, 1),
-            imag_of(0, 2),
-            imag_of(1, 2),
+        def off_real(a, n):
+            return a[2] * n[0] - a[3] * n[1] - (a[0] * n[2] - a[1] * n[3])
+
+        def off_imag(a, n):
+            return a[2] * n[1] + a[3] * n[0] - (a[0] * n[3] + a[1] * n[2])
+
+        first, second, third = stress
+        along, length = unit(first)
+        turn, height = unit([off_real(second, along), off_imag(second, along)])
+        x, y = off_real(third, along), off_imag(third, along)
+        triangle = [
+            length,
+            real_of(second, along),
+            imag_of(second, along),
+            real_of(third, along),
+            imag_of(third, along),
+            height,
+            x * turn[0] + y * turn[1],
+            y * turn[0] - x * turn[1],
         ]
-        for i, value in enumerate(cross):
+        for i, value in enumerate(triangle):
             outgoing[step, i] = value.astype(jnp.bfloat16)
 
         @pl.when(step < PEERS - 1)
         def _():
             copy_s(step).start()
 
-        equivalent = cross[0] + cross[1] - cross[3] + 3.0 * cross[2]
-        r = table[:, 0:1]
+        equivalent = (
+            real_of(first, first)
+            + real_of(second, second)
+            - real_of(first, second)
+            + 3.0 * real_of(third, third)
+        )
         r2 = r * r
         listed = [
             jnp.sum(value, axis=0, keepdims=True)
@@ -298,12 +314,32 @@
     lax.fori_loop(0, PEERS, serve, 0)
     moments_ref[...] = moments_ref[...] / (PEERS * lines)
 
-    keep = pltpu.make_async_copy(outgoing.at[PEERS - 1], spectra_ref.at[:, :, here], load_sem.at[0])
-    keep.start()
-    for step in range(PEERS - 1):
+    def expand(ref, step):
+        at = pl.ds(pl.multiple_of(source(freq, step) * width, width), width)
+        r, br, bi, cr, ci, h, dr, di = (ref[i].astype(jnp.float32) for i in range(8))
+        cross = (
+            r * r,
+            br * br + bi * bi + h * h,
+            cr * cr + ci * ci + (dr * dr + di * di),
+            r * br,
+            r * cr,
+            br * cr + bi * ci + h * dr,
+            -(r * bi),
+            -(r * ci),
+            bi * cr - br * ci - h * di,
+        )
+        for i, value in enumerate(cross):
+            spectra_ref[i, :, at] = value.astype(jnp.bfloat16)
+
+    expand(outgoing.at[PEERS - 1], PEERS - 1)
+
+    def take(step, carry):
         copy_s(step).wait_recv()
-    keep.wait()
-    for copy in (copy_a, copy_f, copy_b, copy_c, copy_s):
+        expand(arrived.at[step], step)
+        return carry
+
+    lax.fori_loop(0, PEERS - 1, take, 0)
+    for copy in (copy_a, copy_b, copy_c, copy_s):
         sent(copy)
 
 
@@ -328,14 +364,15 @@
             *[pltpu.VMEM(a.shape, a.dtype) for a in args],
             pltpu.VMEM((PEERS, 8, LANES), f32),
             pltpu.VMEM((PEERS, 8, LANES), f32),
+            pltpu.VMEM((PEERS, 16, LANES), f32),
             pltpu.VMEM((PEERS, 8, LANES), f32),
-            pltpu.VMEM((PEERS, 8, LANES), f32),
-            pltpu.VMEM((PEERS, lines, LANES), f32),
+            pltpu.VMEM((PEERS, 2 * lines, 8), f32),
             pltpu.VMEM((1, width), f32),
             pltpu.VMEM((4 * lines, num_modes), bf16),
-            pltpu.VMEM((PEERS, 9, lines, width), bf16),
+            pltpu.VMEM((PEERS, 8, lines, width), bf16),
+            pltpu.VMEM((PEERS, 8, lines, width), bf16),
             sems,
-            *[sems] * 10,
+            *[sems] * 8,
         ],
         compiler_params=pltpu.CompilerParams(
             collective_id=0, has_side_effects=True, vmem_limit_bytes=40 << 20

time: 71.1 us -> 67.7 us (0.952)
  Pallas kernels: 68.6 us -> 65.2 us
    pallas_call x1, Pallas kernels: 68.6 us -> 65.2 us  [local(): pl.pallas_call(kernel, out_shape=(jax.ShapeDtypeStruct((9, lines, PEERS *...]
where the time goes in v3:
time: 67.7 us; the launch traced here: 67.6 us
  Pallas kernels  65.2 us (96%)
  local copies, waits for them, and re-layouts  1.8 us (3%)
    pallas_call x1, Pallas kernels, local(): pl.pallas_call(kernel, out_shape=(jax.ShapeDtypeStruct((9, lines, PEERS *...  65.2 us
    unnamed x2, local copies, waits for them, and re-layouts  1.8 us

profile of v3, /device:TPU:1, one launch (start us, length us, event | category | flops | bytes accessed | tf_op | source)
XLA Modules:
  0.0 67.6 jit_solution(2460534444304851517)
XLA Ops:
  0.6 65.2 %shard_map.113 = (bf16[9,24,4096]{2,1,0:T(8,128)(2,1)S(1)}, f32[4,256]{1,0:T(4,128)S(1)}) custom-call(bf16[3,3000,256]{2,1,0:T(8,128)(2,1)} %modes_any.1, f32[16,3000]{1,0:T(8,128)} %shapes_any.1, s32[1,4]{1,0:T(1,128)} %bitcast.11, f32[1,3000]{1,0:T(1,128)} %bitcast.8, f32[1,3000]{1,0:T(1,128)} %bitcast.9, s32[1,24]{1,0:T(1,128)} %bitcast.12, ...), custom_call_target="tpu_custom_call" | custom-call | flops 7100000256 | bytes 10000000 | tf_op jit(solution)/shard_map/pallas_call | solution.py:355
  65.8 1.2 %copy.14 = bf16[24,9,4096]{2,0,1:T(8,128)(2,1)} copy(bf16[24,9,4096]{2,0,1:T(8,128)(2,1)S(1)} %bitcast.7) | data formatting | bytes 3538944
  67.1 0.6 copy.15

commit v4 on v3

--- a/solution.py
+++ b/solution.py
@@ -54,6 +54,12 @@
     x, y, c = ELEM_STEPS[step]
     x_hi, y_at, core = elem // 8, (elem // 2) % 4, elem % 2
     return ((x_hi + x) % 2) * 8 + ((y_at + y) % 4) * 2 + (core + c) % 2
+
+
+def elem_source(elem, step):
+    x, y, c = ELEM_STEPS[step]
+    x_hi, y_at, core = elem // 8, (elem // 2) % 4, elem % 2
+    return ((x_hi + x) % 2) * 8 + ((y_at + 4 - y) % 4) * 2 + (core + c) % 2
 
 
 def kernel(
@@ -197,7 +203,14 @@
         for step in range(PEERS - 1):
             copy(step).wait_send()
 
-    started(copy_a)
+    chunks = (tiles + 1) // 2
+    holds = elem < chunks
+    for step in range(PEERS - 1):
+
+        @pl.when(elem_peer(elem, step) < chunks)
+        def _():
+            copy_a(step).start()
+
     partial[PEERS - 1] = picked[elem]
 
     sets = block[...]
@@ -207,16 +220,28 @@
     scaling[...] = found
     moments_ref[...] = jnp.zeros(moments_ref.shape, jnp.float32)
 
-    received(copy_a)
+    @pl.when(holds)
+    def _():
+        received(copy_a)
+
     summed[PEERS - 1, :8] = jnp.sum(partial[...], axis=0)
     started(copy_b)
     received(copy_b)
     wheels[elem] = jnp.sum(summed[:, :8], axis=0)
-    started(copy_c)
+
+    @pl.when(holds)
+    def _():
+        started(copy_c)
+
     for step in range(PEERS):
         factors[source(freq, step)] = jnp.transpose(summed[step, 8:])[: 2 * lines]
     loads[9].wait()
-    received(copy_c)
+    for step in range(PEERS - 1):
+
+        @pl.when(elem_source(elem, step) < chunks)
+        def _():
+            copy_c(step).wait_recv()
+
 
     def copy_s(step):
         return pltpu.make_async_remote_copy(
@@ -339,8 +364,30 @@
         return carry
 
     lax.fori_loop(0, PEERS - 1, take, 0)
-    for copy in (copy_a, copy_b, copy_c, copy_s):
-        sent(copy)
+    for step in range(PEERS - 1):
+
+        @pl.when(elem_peer(elem, step) < chunks)
+        def _():
+            copy_a(step).wait_send()
+
+    @pl.when(holds)
+    def _():
+        sent(copy_c)
+
+    sent(copy_b)
+    sent(copy_s)
+
+
+def store_kernel(spectra_ref, moments_ref, spectra_out, moments_out, sem):
+    copies = [
+        pltpu.make_async_copy(spectra_ref.at[i], spectra_out.at[i], sem.at[i])
+        for i in range(spectra_ref.shape[0])
+    ]
+    copies.append(pltpu.make_async_copy(moments_ref, moments_out, sem.at[9]))
+    for copy in copies:
+        copy.start()
+    for copy in copies:
+        copy.wait()
 
 
 def local(*args):
@@ -379,6 +426,16 @@
         ),
         cost_estimate=pl.CostEstimate(flops=7_100_000_000, bytes_accessed=10_000_000, transcendentals=0),
     )(*args)
+    spectra, moments = pl.pallas_call(
+        store_kernel,
+        out_shape=(
+            jax.ShapeDtypeStruct(spectra.shape, spectra.dtype),
+            jax.ShapeDtypeStruct(moments.shape, moments.dtype),
+        ),
+        in_specs=[pl.BlockSpec(memory_space=pltpu.VMEM)] * 2,
+        out_specs=[pl.BlockSpec(memory_space=pltpu.HBM)] * 2,
+        scratch_shapes=[pltpu.SemaphoreType.DMA((10,))],
+    )(*[pltpu.with_memory_space_constraint(a, pltpu.VMEM) for a in (spectra, moments)])
     return jnp.transpose(spectra, (1, 0, 2)), moments
 
 

time: 67.7 us -> 66.8 us (0.987)
  local copies, waits for them, and re-layouts: 1.8 us -> 0 us
  Pallas kernels: 65.2 us -> 66 us
    unnamed x2 -> x0, local copies, waits for them, and re-layouts: 1.8 us -> none
    pallas_call x0 -> x1, Pallas kernels: none -> 1.28 us  [local(): pl.pallas_call(store_kernel, out_shape=(jax.ShapeDtypeStruct(spectra.shap...]
where the time goes in v4:
time: 66.8 us; the launch traced here: 66.7 us
  Pallas kernels  66 us (99%)
    pallas_call x1, Pallas kernels, local(): pl.pallas_call(kernel, out_shape=(jax.ShapeDtypeStruct((9, lines, PEERS *...  64.7 us

profile of v4, /device:TPU:1, one launch (start us, length us, event | category | flops | bytes accessed | tf_op | source)
XLA Modules:
  0.0 66.7 jit_solution(6663003305542948819)
XLA Ops:
  0.6 64.7 %shard_map.113 = (bf16[9,24,4096]{2,1,0:T(8,128)(2,1)S(1)}, f32[4,256]{1,0:T(4,128)S(1)}) custom-call(bf16[3,3000,256]{2,1,0:T(8,128)(2,1)} %modes_any.1, f32[16,3000]{1,0:T(8,128)} %shapes_any.1, s32[1,4]{1,0:T(1,128)} %bitcast.11, f32[1,3000]{1,0:T(1,128)} %bitcast.8, f32[1,3000]{1,0:T(1,128)} %bitcast.9, s32[1,24]{1,0:T(1,128)} %bitcast.12, ...), custom_call_target="tpu_custom_call" | custom-call | flops 7100000256 | bytes 10000000 | tf_op jit(solution)/shard_map/pallas_call | solution.py:402
  65.4 1.3 %shard_map.114 = (bf16[9,24,4096]{2,1,0:T(8,128)(2,1)}, f32[4,256]{1,0:T(4,128)}) custom-call(bf16[9,24,4096]{2,1,0:T(8,128)(2,1)S(1)} %get-tuple-element.6.spectra_ref, f32[4,256]{1,0:T(4,128)S(1)} %get-tuple-element.7.moments_ref), custom_call_target="tpu_custom_call" | custom-call | tf_op jit(solution)/shard_map/pallas_call | solution.py:429

commit v5 on v4

--- a/solution.py
+++ b/solution.py
@@ -88,6 +88,7 @@
     picked,
     partial,
     summed,
+    packs,
     wheels,
     factors,
     scaling,
@@ -103,6 +104,8 @@
     recv_c,
     send_s,
     recv_s,
+    send_f,
+    recv_f,
 ):
     elem = lax.axis_index("elem")
     freq = lax.axis_index("freq")
@@ -156,7 +159,7 @@
     waves = jnp.concatenate([amplitude * jnp.cos(angle), amplitude * jnp.sin(angle)], axis=0)
     ratios = jnp.concatenate([ratio, jnp.zeros((7, lines), jnp.float32)], axis=0)
     rest = jnp.zeros((8, LANES - 2 * lines), jnp.float32)
-    summed[PEERS - 1, 8:] = jnp.concatenate([waves, ratios, rest], axis=1)
+    packs[PEERS - 1] = jnp.concatenate([waves, ratios, rest], axis=1)
 
     pl.semaphore_wait(barrier, 2 * (PEERS - 1))
 
@@ -171,6 +174,16 @@
             device_id_type=MESH,
         )
 
+    def copy_f(step):
+        return pltpu.make_async_remote_copy(
+            src_ref=packs.at[PEERS - 1],
+            dst_ref=packs.at[step],
+            send_sem=send_f.at[step],
+            recv_sem=recv_f.at[step],
+            device_id=(elem, partner(freq, step)),
+            device_id_type=MESH,
+        )
+
     def copy_b(step):
         return pltpu.make_async_remote_copy(
             src_ref=summed.at[PEERS - 1],
@@ -211,6 +224,7 @@
         def _():
             copy_a(step).start()
 
+    started(copy_f)
     partial[PEERS - 1] = picked[elem]
 
     sets = block[...]
@@ -223,18 +237,15 @@
     @pl.when(holds)
     def _():
         received(copy_a)
-
-    summed[PEERS - 1, :8] = jnp.sum(partial[...], axis=0)
-    started(copy_b)
-    received(copy_b)
-    wheels[elem] = jnp.sum(summed[:, :8], axis=0)
-
-    @pl.when(holds)
-    def _():
+        summed[PEERS - 1] = jnp.sum(partial[...], axis=0)
+        started(copy_b)
+        received(copy_b)
+        wheels[elem] = jnp.sum(summed[...], axis=0)
         started(copy_c)
 
+    received(copy_f)
     for step in range(PEERS):
-        factors[source(freq, step)] = jnp.transpose(summed[step, 8:])[: 2 * lines]
+        factors[source(freq, step)] = jnp.transpose(packs[step])[: 2 * lines]
     loads[9].wait()
     for step in range(PEERS - 1):
 
@@ -372,9 +383,10 @@
 
     @pl.when(holds)
     def _():
+        sent(copy_b)
         sent(copy_c)
 
-    sent(copy_b)
+    sent(copy_f)
     sent(copy_s)
 
 
@@ -411,7 +423,8 @@
             *[pltpu.VMEM(a.shape, a.dtype) for a in args],
             pltpu.VMEM((PEERS, 8, LANES), f32),
             pltpu.VMEM((PEERS, 8, LANES), f32),
-            pltpu.VMEM((PEERS, 16, LANES), f32),
+            pltpu.VMEM((PEERS, 8, LANES), f32),
+            pltpu.VMEM((PEERS, 8, LANES), f32),
             pltpu.VMEM((PEERS, 8, LANES), f32),
             pltpu.VMEM((PEERS, 2 * lines, 8), f32),
             pltpu.VMEM((1, width), f32),
@@ -419,7 +432,7 @@
             pltpu.VMEM((PEERS, 8, lines, width), bf16),
             pltpu.VMEM((PEERS, 8, lines, width), bf16),
             sems,
-            *[sems] * 8,
+            *[sems] * 10,
         ],
         compiler_params=pltpu.CompilerParams(
             collective_id=0, has_side_effects=True, vmem_limit_bytes=40 << 20

time: 66.8 us -> 66.2 us (level)
  no operation moved by 1% of the time
where the time goes in v5:
time: 66.2 us
  Pallas kernels  65.5 us (99%)
    pallas_call x1, Pallas kernels, local(): pl.pallas_call(kernel, out_shape=(jax.ShapeDtypeStruct((9, lines, PEERS *...  64.2 us

profile of v5, /device:TPU:1, one launch (start us, length us, event | category | flops | bytes accessed | tf_op | source)
XLA Modules:
  0.0 66.2 jit_solution(11757156469508381969)
XLA Ops:
  0.6 64.2 %shard_map.113 = (bf16[9,24,4096]{2,1,0:T(8,128)(2,1)S(1)}, f32[4,256]{1,0:T(4,128)S(1)}) custom-call(bf16[3,3000,256]{2,1,0:T(8,128)(2,1)} %modes_any.1, f32[16,3000]{1,0:T(8,128)} %shapes_any.1, s32[1,4]{1,0:T(1,128)} %bitcast.11, f32[1,3000]{1,0:T(1,128)} %bitcast.8, f32[1,3000]{1,0:T(1,128)} %bitcast.9, s32[1,24]{1,0:T(1,128)} %bitcast.12, ...), custom_call_target="tpu_custom_call" | custom-call | flops 7100000256 | bytes 10000000 | tf_op jit(solution)/shard_map/pallas_call | solution.py:414
  64.9 1.3 %shard_map.114 = (bf16[9,24,4096]{2,1,0:T(8,128)(2,1)}, f32[4,256]{1,0:T(4,128)}) custom-call(bf16[9,24,4096]{2,1,0:T(8,128)(2,1)S(1)} %get-tuple-element.6.spectra_ref, f32[4,256]{1,0:T(4,128)S(1)} %get-tuple-element.7.moments_ref), custom_call_target="tpu_custom_call" | custom-call | tf_op jit(solution)/shard_map/pallas_call | solution.py:442

commit v6 on v5

--- a/solution.py
+++ b/solution.py
@@ -392,8 +392,10 @@
 
 def store_kernel(spectra_ref, moments_ref, spectra_out, moments_out, sem):
     copies = [
-        pltpu.make_async_copy(spectra_ref.at[i], spectra_out.at[i], sem.at[i])
-        for i in range(spectra_ref.shape[0])
+        pltpu.make_async_copy(
+            spectra_ref.at[pl.ds(3 * i, 3)], spectra_out.at[pl.ds(3 * i, 3)], sem.at[i]
+        )
+        for i in range(spectra_ref.shape[0] // 3)
     ]
     copies.append(pltpu.make_async_copy(moments_ref, moments_out, sem.at[9]))
     for copy in copies:

time: 66.2 us -> 66.3 us (level)
  no operation moved by 1% of the time
where the time goes in v6:
time: 66.3 us; the launch traced here: 66.2 us
  Pallas kernels  65.5 us (99%)
    pallas_call x1, Pallas kernels, local(): pl.pallas_call(kernel, out_shape=(jax.ShapeDtypeStruct((9, lines, PEERS *...  64.2 us

profile of v6, /device:TPU:1, one launch (start us, length us, event | category | flops | bytes accessed | tf_op | source)
XLA Modules:
  0.0 66.2 jit_solution(6880759884230654640)
XLA Ops:
  0.6 64.2 %shard_map.113 = (bf16[9,24,4096]{2,1,0:T(8,128)(2,1)S(1)}, f32[4,256]{1,0:T(4,128)S(1)}) custom-call(bf16[3,3000,256]{2,1,0:T(8,128)(2,1)} %modes_any.1, f32[16,3000]{1,0:T(8,128)} %shapes_any.1, s32[1,4]{1,0:T(1,128)} %bitcast.11, f32[1,3000]{1,0:T(1,128)} %bitcast.8, f32[1,3000]{1,0:T(1,128)} %bitcast.9, s32[1,24]{1,0:T(1,128)} %bitcast.12, ...), custom_call_target="tpu_custom_call" | custom-call | flops 7100000256 | bytes 10000000 | tf_op jit(solution)/shard_map/pallas_call | solution.py:416
  64.9 1.3 %shard_map.114 = (bf16[9,24,4096]{2,1,0:T(8,128)(2,1)}, f32[4,256]{1,0:T(4,128)}) custom-call(bf16[9,24,4096]{2,1,0:T(8,128)(2,1)S(1)} %get-tuple-element.6.spectra_ref, f32[4,256]{1,0:T(4,128)S(1)} %get-tuple-element.7.moments_ref), custom_call_target="tpu_custom_call" | custom-call | tf_op jit(solution)/shard_map/pallas_call | solution.py:444
